TPU v7x, 128 devices: a whole 4x4x4 slice. The times are simulated.
128 devices in a mesh: mom: 8 (over y, core), pair: 16 (over x, z).
Axes of the slice: x: 4, y: 4, z: 4, core: 2. Of those that a mesh axis runs over, the one named last changes fastest.
Arguments:
- blocks: bfloat16 [8, 16, 1024, 1024], P('mom', None, 'pair'), may hold values from -1.078125 to 1.078125
- left_ids: int32 [8, 48], P('mom', 'pair'), may hold values from 0 to 15
- right_ids: int32 [8, 48], P('mom', 'pair'), may hold values from 0 to 15
- slice_ids: int32 [8, 48], P('mom', 'pair'), may hold values from 0 to 1
- weight_ids: int32 [8, 48], P('mom', 'pair'), may hold values from 0 to 7
- counts: int32 [8, 16], P('mom', 'pair'), may hold values from 1 to 3, 32 in all within a row
- subduction: float32 [8], replicated, may hold values from -1 to 1
Outputs:
- operator: float32 [8, 1024, 2, 1024], P('mom', 'pair')
Inputs may be any that keep to these rules, and one draw needn't show every extreme that they name: Each row of counts sums to exactly 32.
All inputs are finite; a program needn't handle non-finite values. No bound on the sum of `counts` on one device may be relied on, other than what follows from the above.
Results may differ from a plain program's by a relative error of at most 0.0029.
Values may be sent and summed in bfloat16 or wider, within the bound.
A program may use at most 128 MiB of HBM per device.

v0:
```python
import jax
import jax.numpy as jnp
from jax import lax
from jax.sharding import PartitionSpec as P

PAIR_DEV = 3
SLICES = 2


def partner_2(shard, axis, apart):
    return lax.ppermute(shard, axis, [(i, i ^ 1 << apart) for i in range(lax.axis_size(axis))])


def mixing_table(lefts, rights, slices, weights, allowed, subduction, families):
    total_slots = lefts.shape[0]
    slot = jnp.arange(total_slots, dtype=jnp.int32)
    list_of = slot // PAIR_DEV
    lists = jnp.arange(allowed.shape[0], dtype=jnp.int32)
    limit = jnp.sum(jnp.where(list_of[:, None] == lists[None, :], allowed[None, :], 0), axis=1)
    live = slot % PAIR_DEV < limit
    table_ids = jnp.arange(subduction.shape[0], dtype=jnp.int32)
    looked = jnp.sum(
        jnp.where(weights[:, None] == table_ids[None, :], subduction[None, :], 0.0), axis=1
    )
    select = (slices[:, None] == jnp.arange(SLICES, dtype=jnp.int32)[None, :]).astype(jnp.float32)
    scales = jnp.where(live, looked, 0.0)[:, None] * select
    fam_ids = jnp.arange(families, dtype=jnp.int32)
    right_hot = (rights[:, None] == fam_ids[None, :]).astype(jnp.float32)
    left_hot = (lefts[:, None] == fam_ids[None, :]).astype(jnp.float32)
    return jnp.einsum("kt,kb,ka->tba", scales, right_hot, left_hot, precision=lax.Precision.HIGHEST)


def combine_left(mixing, panels):
    families = panels.shape[0]
    flat = panels.astype(jnp.float32).reshape(families, -1)
    mixed = jnp.dot(
        mixing.reshape(SLICES * families, families), flat, precision=lax.Precision.HIGHEST
    )
    return mixed.astype(jnp.bfloat16).reshape((SLICES, families) + panels.shape[1:])


def body(blocks, left_ids, right_ids, slice_ids, weight_ids, counts, subduction):
    gathered = (
        lax.all_gather(left_ids, "pair", axis=1, tiled=True),
        lax.all_gather(right_ids, "pair", axis=1, tiled=True),
        lax.all_gather(slice_ids, "pair", axis=1, tiled=True),
        lax.all_gather(weight_ids, "pair", axis=1, tiled=True),
        lax.all_gather(counts, "pair", axis=1, tiled=True),
    )
    own = blocks[0]
    families = own.shape[0]
    mixing = mixing_table(
        gathered[0][0],
        gathered[1][0],
        gathered[2][0],
        gathered[3][0],
        gathered[4][0],
        subduction,
        families,
    )
    partner = partner_2(own, "mom", 0)
    combined = combine_left(mixing, own)
    result = jnp.einsum(
        "tbij,bjl->itl",
        combined,
        lax.all_gather(partner, "pair", axis=1, tiled=True),
        preferred_element_type=jnp.float32,
    )
    return result.reshape((1,) + result.shape)


def solution(mesh):
    return jax.shard_map(
        body,
        mesh=mesh,
        in_specs=(
            P("mom", None, "pair", None),
            P("mom", "pair"),
            P("mom", "pair"),
            P("mom", "pair"),
            P("mom", "pair"),
            P("mom", "pair"),
            P(),
        ),
        out_specs=P("mom", "pair", None, None),
        check_vma=False,
    )
```

profile of v0, /device:TPU:1, one launch (start us, length us, event | category | flops | bytes accessed | tf_op | source)
XLA Modules:
  0.0 235.2 jit_solution(4597328169797305027)
XLA Ops:
  6.5 0.0 copy-start.5
  6.6 0.0 all-gather.2.cloned.1.call-start
  6.6 1.5 collective-permute-start
  8.1 4.0 %collective-permute-done = bf16[16,64,1024]{2,1,0:T(8,128)(2,1)S(1)} collective-permute-done((bf16[16,64,1024]{2,1,0:T(8,128)(2,1)}, bf16[16,64,1024]{2,1,0:T(8,128)(2,1)S(1)}, u32[]{:S(2)}, u32[]{:S(2)}) %collective-permute-start) | collective-permute-done | bytes 2097184 | tf_op jit(solution)/shard_map/ppermute | solution.py:11
  12.1 1.3 copy-done
  13.4 0.0 all-gather.2.cloned.1.call-update
  14.1 2.7 %copy.11 = bf16[2,8,64,1024]{3,1,2,0:T(8,128)(2,1)S(1)} copy(bf16[2,8,64,1024]{3,2,1,0:T(8,128)(2,1)} %bitcast.49) | data formatting | bytes 4194304
  16.8 0.0 copy-done.6
  16.9 0.6 dynamic-slice
  18.1 0.7 bitcast_dynamic-update-slice_fusion.2
  18.8 0.0 copy-done.1
  18.8 0.1 bitcast_dynamic-update-slice_fusion.4
  18.9 0.1 bitcast_dynamic-update-slice_fusion.1
  19.0 0.1 bitcast_dynamic-update-slice_fusion.3
  19.1 0.1 bitcast_dynamic-update-slice_fusion
  19.2 13.6 %all-reduce.5 = (s32[48]{0:T(128)S(1)}, s32[48]{0:T(128)S(1)}, s32[16]{0:T(128)S(1)}, s32[48]{0:T(128)S(1)}, s32[48]{0:T(128)S(1)}) all-reduce(s32[48]{0:T(128)S(1)} %bitcast_dynamic-update-slice_fusion.3, s32[48]{0:T(128)S(1)} %bitcast_dynamic-update-slice_fusion.1, ...), channel_id=1, replica_groups=mesh['mom'=8,'pair'=16] {'pair'}, use_global_device_ids=true, to_apply=%add.1 | all-reduce | flops 208 | bytes 1664
  32.9 0.1 select_reduce_fusion.1
  32.9 0.1 select_reduce_fusion
  33.1 0.1 fusion.8
  33.2 3.6 %convolution_convert_fusion = bf16[32,65536]{1,0:T(8,128)(2,1)S(1)} fusion(f32[32,16]{1,0:T(8,128)S(1)} %bitcast.50, bf16[16,65536]{1,0:T(8,128)(2,1)S(1)} %bitcast.47), kind=kOutput, calls=%fused_computation | convolution fusion | flops 404750336 | bytes 6293504 | tf_op jit(solution)/shard_map/dot_general | solution.py:36
  36.8 4.4 %copy.12 = bf16[4,8,64,1024]{3,2,1,0:T(8,128)(2,1)} copy(bf16[4,8,64,1024]{3,1,2,0:T(8,128)(2,1)S(1)} %bitcast.46) | data formatting | bytes 8388608
  41.1 171.9 %all-gather.2.cloned.1.call-done = bf16[16,1024,1024]{2,1,0:T(8,128)(2,1)} async-done(((bf16[16,64,1024]{2,1,0:T(8,128)(2,1)}), bf16[16,1024,1024]{2,1,0:T(8,128)(2,1)}) %all-gather.2.cloned.1.call-update) | async-done | bytes 33554448 | tf_op jit(solution)/shard_map/all_gather | solution.py:66
  213.0 14.1 %fusion.3 = f32[1,64,2,1024]{3,1,2,0:T(8,128)S(1)} fusion(bf16[16,1024,1024]{2,1,0:T(8,128)(2,1)} %all-gather.2.cloned.1.call-done, bf16[2,16,64,1024]{3,2,1,0:T(8,128)(2,1)} %bitcast.45), kind=kOutput, calls=%fused_computation.4 | convolution fusion | flops 4294967296 | bytes 38273024 | tf_op jit(solution)/shard_map/tbij,bjl->itl/dot_general | solution.py:63
  227.1 1.2 copy.9
  (19 shorter events, 0.1 us)
Async XLA Ops:
  6.5 10.3 %copy-start.6 = (u32[128]{0:T(128)S(1)}, u32[128]{0:T(128)}, u32[]{:S(2)}) copy-start(u32[128]{0:T(128)} %constant.32) | copy-start | bytes 1540
  6.5 12.3 %copy-start.1 = (s32[1,3]{1,0:T(1,128)S(1)}, s32[1,3]{1,0:T(1,128)}, u32[]{:S(2)}) copy-start(s32[1,3]{1,0:T(1,128)} %param.9) | copy-start | bytes 40
  6.5 12.4 %copy-start.2 = (s32[1,3]{1,0:T(1,128)S(1)}, s32[1,3]{1,0:T(1,128)}, u32[]{:S(2)}) copy-start(s32[1,3]{1,0:T(1,128)} %param.11) | copy-start | bytes 40
  6.5 12.5 %copy-start.3 = (s32[1,3]{1,0:T(1,128)S(1)}, s32[1,3]{1,0:T(1,128)}, u32[]{:S(2)}) copy-start(s32[1,3]{1,0:T(1,128)} %param.10) | copy-start | bytes 40
  6.5 12.6 %copy-start.4 = (s32[1,3]{1,0:T(1,128)S(1)}, s32[1,3]{1,0:T(1,128)}, u32[]{:S(2)}) copy-start(s32[1,3]{1,0:T(1,128)} %param.8) | copy-start | bytes 40
  6.5 26.3 %copy-start.5 = (f32[8]{0:T(128)S(1)}, f32[8]{0:T(128)}, u32[]{:S(2)}) copy-start(f32[8]{0:T(128)} %param.13) | copy-start | bytes 100
  6.6 206.5 %all-gather.2.cloned.1.call-start = ((), (), s32[]{:S(2)}) async-start(), calls=%async_computation | async-start | bytes 35651584 | tf_op jit(solution)/shard_map/all_gather | solution.py:66
  6.6 5.5 %collective-permute-start = (bf16[16,64,1024]{2,1,0:T(8,128)(2,1)}, bf16[16,64,1024]{2,1,0:T(8,128)(2,1)S(1)}, u32[]{:S(2)}, u32[]{:S(2)}) collective-permute-start(bf16[16,64,1024]{2,1,0:T(8,128)(2,1)} %bitcast.48), channel_id=1, source_target_pairs={{0,16},{16,0},{32,48},{48,32},{64,80},{80,64},{96,112},{112,96},{1... | collective-permute-start | bytes 6291464 | tf_op jit(solution)/shard_map/ppermute | solution.py:11
  12.1 1.3 copy-start
Sparse Core Ops, SparseCore 0:
  13.6 199.4 all-gather.1
where the time goes:
time: 235 us
  waiting for transfers between devices  176 us (75%)
  matrix products  17.8 us (8%)
  between operations  14.8 us (6%)
  blocking collectives  13.6 us (6%)
  local copies, waits for them, and re-layouts  11.3 us (5%)
    all_gather x1, waiting for transfers between devices, body(): lax.all_gather(partner, 'pair', axis=1, tiled=True)  172 us
    dot_general x1, matrix products, body(): jnp.einsum('tbij,bjl->itl', combined, lax.all_gather(partner, 'pair', axi...  14.1 us
    unnamed x1, blocking collectives  13.6 us
    unnamed x27, local copies, waits for them, and re-layouts  10.1 us
  transfers between devices with their start and end apart: 2, of which 2 were waited for; matrix products, arithmetic and copies ran while one was open for 5% of the time, Pallas kernels for 0%

commit v1 on v0

v1 whole, which is shorter than its diff:
```python
import functools

import jax
import jax.numpy as jnp
from jax import lax
from jax.experimental import pallas as pl
from jax.experimental.pallas import tpu as pltpu
from jax.sharding import PartitionSpec as P

MESH = pl.DeviceIdType.MESH
PAIR_DEV = 3
SLICES = 2
FAM = 16
ROWS = 64
LANES = 128
ORDER = 1024
DEVS = 16
OUT_ROWS = SLICES * ROWS
MIX = SLICES * FAM
SUB = 16
CHUNK = 256
NCHUNK = ORDER // CHUNK

PEERS = ((0, 0), (0, 1), (1, 0), (3, 0), (1, 1), (3, 1), (2, 0), (2, 1))


def kernel(
    left, right, slices, weights, counts, subduction, blocks, out,
    rows_b, parts_a, combined, partial, landed, table, tile, tiles, spread,
    own_sem, tile_send, tile_recv, a_send, a_recv, b_send, b_recv, c_send, c_recv,
):
    mom, pair = lax.axis_index("mom"), lax.axis_index("pair")
    other = mom + 1 - 2 * lax.rem(mom, 2)
    x, z = lax.div(pair, 4), lax.rem(pair, 4)
    odd = lax.rem(z, 2)
    across = pair + 1 - 2 * odd

    def peer(k, sign):
        dx, dz = PEERS[k]
        to_x = lax.rem(x + sign * dx + 4, 4)
        return to_x * 4 + (3 - z if dz else z)

    barrier = pltpu.get_barrier_semaphore()
    for p in range(DEVS):
        pl.semaphore_signal(barrier, 1, device_id=(other, p), device_id_type=MESH)
    pl.semaphore_signal(barrier, 1, device_id=(mom, across), device_id_type=MESH)

    mine = pl.ds(pl.multiple_of(odd * ROWS, ROWS), ROWS)
    own = pltpu.make_async_copy(blocks.at[0], rows_b.at[:, mine, :], own_sem)
    own.start()

    row = lax.broadcasted_iota(jnp.int32, (8, LANES), 0)
    keys = jnp.zeros((8, LANES), jnp.int32)
    coefs = jnp.zeros((8, LANES), jnp.float32)
    for s in range(PAIR_DEV):
        key = (slices[0, s] * FAM + right[0, s]) * FAM + left[0, s]
        coef = jnp.where(s < counts[0, 0], subduction[weights[0, s]], 0.0)
        keys = jnp.where(row == s, key, keys)
        coefs = jnp.where(row == 4 + s, coef, coefs)
    tile[...] = jnp.where(row < 4, keys.astype(jnp.float32), coefs)

    pl.semaphore_wait(barrier, DEVS + 1)
    sends = []
    for p in range(DEVS):
        copy = pltpu.make_async_remote_copy(
            tile, tiles.at[pair], tile_send.at[p], tile_recv.at[pair],
            device_id=(other, p), device_id_type=MESH,
        )
        copy.start()
        sends.append(copy)

    own.wait()
    gets_a = []
    for k in range(len(PEERS)):
        to = peer(k, 1)
        columns = pl.ds(pl.multiple_of(lax.div(to, 2) * LANES, LANES), LANES)
        copy = pltpu.make_async_remote_copy(
            rows_b.at[:, mine, columns], parts_a.at[k], a_send.at[k], a_recv.at[k],
            device_id=(other, to), device_id_type=MESH,
        )
        copy.start()
        sends.append(copy)
        gets_a.append(copy)
    gets_b = []
    for n in range(NCHUNK):
        part = rows_b.at[:, mine, pl.ds(n * CHUNK, CHUNK)]
        copy = pltpu.make_async_remote_copy(
            part, part, b_send.at[n], b_recv.at[n],
            device_id=(mom, across), device_id_type=MESH,
        )
        copy.start()
        sends.append(copy)
        theirs = pl.ds(pl.multiple_of((1 - odd) * ROWS, ROWS), ROWS)
        part = rows_b.at[:, theirs, pl.ds(n * CHUNK, CHUNK)]
        gets_b.append(pltpu.make_async_copy(part, part, b_recv.at[n]))

    place = lax.broadcasted_iota(jnp.int32, (MIX, LANES), 0) * FAM
    place = place + lax.div(lax.broadcasted_iota(jnp.int32, (MIX, LANES), 1), SUB)
    place_lo = place.astype(jnp.float32)
    place_hi = (place + LANES // SUB).astype(jnp.float32)
    lo = jnp.zeros((MIX, LANES), jnp.float32)
    hi = jnp.zeros((MIX, LANES), jnp.float32)
    for p in range(DEVS):
        pltpu.make_async_copy(tile, tiles.at[p], tile_recv.at[p]).wait()
    for p in range(DEVS):
        for s in range(PAIR_DEV):
            key = tiles[p, s : s + 1, :]
            coef = tiles[p, 4 + s : 5 + s, :]
            lo = lo + jnp.where(place_lo == key, coef, 0.0)
            hi = hi + jnp.where(place_hi == key, coef, 0.0)
    rest = jnp.concatenate([lo, hi], axis=1)
    diagonal = lax.broadcasted_iota(jnp.int32, (SUB, FAM * SUB), 0) == lax.rem(
        lax.broadcasted_iota(jnp.int32, (SUB, FAM * SUB), 1), SUB
    )
    for level in range(3):
        part = rest.astype(jnp.bfloat16).astype(jnp.float32)
        rest = rest - part
        spread[level] = part
    for level in range(3):
        for r in range(MIX):
            square = jnp.where(diagonal, spread[level, r : r + 1, :], 0.0)
            table[r * SUB : (r + 1) * SUB, level * FAM * SUB : (level + 1) * FAM * SUB] = (
                square.astype(jnp.bfloat16)
            )

    for k in range(len(PEERS)):
        gets_a[k].wait_recv()

        @pl.loop(0, ROWS // (2 * SUB))
        def _(h):
            base = pl.multiple_of(h * 2 * SUB, 2 * SUB)
            both = parts_a[k, :, pl.ds(base, 2 * SUB), :]
            first = both[:, :SUB, :].reshape(FAM * SUB, LANES)
            second = both[:, SUB:, :].reshape(FAM * SUB, LANES)
            wide = jnp.concatenate([first, second], axis=1)
            mixed = jnp.dot(
                table[...],
                jnp.concatenate([wide, wide, wide], axis=0),
                preferred_element_type=jnp.float32,
            ).astype(jnp.bfloat16)
            for r in range(MIX):
                t, b = divmod(r, FAM)
                for e in range(2):
                    combined[
                        pl.ds(k * OUT_ROWS + t * ROWS + base + e * SUB, SUB),
                        b * LANES : (b + 1) * LANES,
                    ] = mixed[r * SUB : (r + 1) * SUB, e * LANES : (e + 1) * LANES]

    gets_c = {}

    def reduce(n):
        total = jnp.zeros((OUT_ROWS, CHUNK), jnp.float32)
        for k in range(len(PEERS)):
            gets_c[n, k].wait_recv()
            total = total + landed[n, k].astype(jnp.float32)
        out[:, n * CHUNK : (n + 1) * CHUNK] = total

    for n in range(NCHUNK):
        gets_b[n].wait()
        for k in range(len(PEERS)):
            partial[n, k] = jnp.dot(
                combined[k * OUT_ROWS : (k + 1) * OUT_ROWS, :],
                rows_b[:, :, n * CHUNK : (n + 1) * CHUNK].reshape(FAM * LANES, CHUNK),
                preferred_element_type=jnp.float32,
            ).astype(jnp.bfloat16)
            copy = pltpu.make_async_remote_copy(
                partial.at[n, k], landed.at[n, k], c_send.at[n, k], c_recv.at[n, k],
                device_id=(other, peer(k, -1)), device_id_type=MESH,
            )
            copy.start()
            sends.append(copy)
            gets_c[n, k] = copy
        if n > 0:
            reduce(n - 1)
    reduce(NCHUNK - 1)
    for copy in sends:
        copy.wait_send()


def body(blocks, left_ids, right_ids, slice_ids, weight_ids, counts, subduction):
    bf16, f32 = jnp.bfloat16, jnp.float32
    peers = len(PEERS)
    dma = pltpu.SemaphoreType.DMA
    result = pl.pallas_call(
        kernel,
        out_shape=jax.ShapeDtypeStruct((OUT_ROWS, ORDER), f32),
        in_specs=[pl.BlockSpec(memory_space=pltpu.SMEM)] * 6
        + [pl.BlockSpec(memory_space=pl.ANY)],
        out_specs=pl.BlockSpec(memory_space=pltpu.VMEM),
        scratch_shapes=[
            pltpu.VMEM((FAM, 2 * ROWS, ORDER), bf16),
            pltpu.VMEM((peers, FAM, ROWS, LANES), bf16),
            pltpu.VMEM((peers * OUT_ROWS, FAM * LANES), bf16),
            pltpu.VMEM((NCHUNK, peers, OUT_ROWS, CHUNK), bf16),
            pltpu.VMEM((NCHUNK, peers, OUT_ROWS, CHUNK), bf16),
            pltpu.VMEM((MIX * SUB, 3 * FAM * SUB), bf16),
            pltpu.VMEM((8, LANES), f32),
            pltpu.VMEM((DEVS, 8, LANES), f32),
            pltpu.VMEM((3, MIX, FAM * SUB), f32),
            dma, dma((DEVS,)), dma((DEVS,)), dma((peers,)), dma((peers,)),
            dma((NCHUNK,)), dma((NCHUNK,)), dma((NCHUNK, peers)), dma((NCHUNK, peers)),
        ],
        compiler_params=pltpu.CompilerParams(
            collective_id=0, has_side_effects=True, vmem_limit_bytes=60 << 20
        ),
        cost_estimate=pl.CostEstimate(
            flops=8 << 30, bytes_accessed=4 << 20, transcendentals=0
        ),
    )(left_ids, right_ids, slice_ids, weight_ids, counts, subduction, blocks)
    result = jnp.transpose(result.reshape(SLICES, ROWS, ORDER), (1, 0, 2))
    return result[None]


def solution(mesh):
    return jax.shard_map(
        body,
        mesh=mesh,
        in_specs=(
            P("mom", None, "pair", None),
            P("mom", "pair"),
            P("mom", "pair"),
            P("mom", "pair"),
            P("mom", "pair"),
            P("mom", "pair"),
            P(),
        ),
        out_specs=P("mom", "pair", None, None),
        check_vma=False,
    )
```

time: 235 us -> 74.3 us (0.32)
  waiting for transfers between devices: 176 us -> 0 us
  Pallas kernels: 0 us -> 71.2 us
  matrix products: 17.8 us -> 0 us
  between operations: 14.8 us -> 0.66 us
  blocking collectives: 13.6 us -> 0 us
  local copies, waits for them, and re-layouts: 11.3 us -> 2.24 us
    all_gather x1 -> x0, waiting for transfers between devices: 172 us -> none  [body(): lax.all_gather(partner, 'pair', axis=1, tiled=True)]
    pallas_call x0 -> x1, Pallas kernels: none -> 71.2 us  [body(): pl.pallas_call(kernel, out_shape=jax.ShapeDtypeStruct((OUT_ROWS, ORDER),...]
    dot_general x3 -> x0, matrix products: 17.8 us -> none  [the longest x1 14.1 us: body(): jnp.einsum('tbij,bjl->itl', combined, lax.all_gather(partner, 'pair', axi...]
    unnamed x1 -> x0, blocking collectives: 13.6 us -> none
    unnamed x27 -> x0, local copies, waits for them, and re-layouts: 10.1 us -> none
    ppermute x1 -> x0, waiting for transfers between devices: 4 us -> none  [partner_2(): lax.ppermute(shard, axis, [(i, i ^ 1 << apart) for i in range(lax.axis_si...]
  transfers between devices with their start and end apart: 2 -> 0, of which waited for: 2 -> 0; matrix products, arithmetic and copies ran while one was open for 5% -> 0% of each run, Pallas kernels for 0% -> 0%
where the time goes in v1:
time: 74.3 us; the launch traced here: 74.1 us
  Pallas kernels  71.2 us (96%)
  local copies, waits for them, and re-layouts  2.24 us (3%)
    pallas_call x1, Pallas kernels, body(): pl.pallas_call(kernel, out_shape=jax.ShapeDtypeStruct((OUT_ROWS, ORDER),...  71.2 us
    reshape x1, local copies, waits for them, and re-layouts, body(): result = jnp.transpose(result.reshape(SLICES, ROWS, ORDER), (1, 0, 2))  2.24 us

profile of v1, /device:TPU:1, one launch (start us, length us, event | category | flops | bytes accessed | tf_op | source)
XLA Modules:
  0.0 74.1 jit_solution(2514131282751736595)
XLA Ops:
  0.7 71.2 %shard_map.73 = f32[128,1024]{1,0:T(8,128)} custom-call(s32[1,3]{1,0:T(1,128)} %left.1, s32[1,3]{1,0:T(1,128)} %right.1, s32[1,3]{1,0:T(1,128)} %slices.1, s32[1,3]{1,0:T(1,128)} %weights.1, s32[1,1]{1,0:T(1,128)S(6)} %copy.11.counts, f32[8]{0:T(128)} %subduction.1, bf16[1,16,64,1024]{3,2,1,0:T(8,128)(2,1)} %blocks.1), custom_call_target="tpu_custom_call" | custom-call | flops 8589934592 | bytes 4194304 | tf_op jit(solution)/shard_map/pallas_call | solution.py:184
  71.9 2.2 %copy.10 = f32[2,64,1024]{2,0,1:T(2,128)} copy(f32[2,64,1024]{2,1,0:T(8,128)} %bitcast.6) | data formatting | bytes 1048576 | tf_op jit(solution)/shard_map/reshape | solution.py:210

commit v2 on v1

v2 whole, which is shorter than its diff:
```python
import functools

import jax
import jax.numpy as jnp
from jax import lax
from jax.experimental import pallas as pl
from jax.experimental.pallas import tpu as pltpu
from jax.sharding import PartitionSpec as P

MESH = pl.DeviceIdType.MESH
PAIR_DEV = 3
SLICES = 2
FAM = 16
ROWS = 64
LANES = 128
ORDER = 1024
DEVS = 16
OUT_ROWS = SLICES * ROWS
MIX = SLICES * FAM
SUB = 16
DOT_ROWS = 256
CHUNKS = ((0, 256), (256, 256), (512, 256), (768, 128), (896, 128))

PEERS = ((0, 0), (0, 1), (1, 0), (3, 0), (2, 0), (1, 1), (3, 1), (2, 1))
SLOT = {peer: k for k, peer in enumerate(PEERS)}


def kernel(
    left_in, right_in, slices_in, weights_in, counts_in, subduction_in, blocks, out,
    left, right, slices, weights, counts, subduction,
    rows_b, parts_a, relay, combined, partial, landed,
    table, tile, tiles, spread,
    small_sem, own_sem, tile_send, tile_recv, a_send, a_recv, relay_send, relay_recv,
    b_send, b_recv, c_send, c_recv,
):
    mom, pair = lax.axis_index("mom"), lax.axis_index("pair")
    other = mom + 1 - 2 * lax.rem(mom, 2)
    x, z = lax.div(pair, 4), lax.rem(pair, 4)
    odd = lax.rem(z, 2)
    across = pair + 1 - 2 * odd

    def at(dx, dz):
        return lax.rem(x + dx + 4, 4) * 4 + (3 - z if dz else z)

    friends = [(other, p) for p in range(DEVS)]
    friends += [(mom, across), (mom, at(0, 1))]
    barrier = pltpu.get_barrier_semaphore()
    for friend in friends:
        pl.semaphore_signal(barrier, 1, device_id=friend, device_id_type=MESH)

    mine = pl.ds(pl.multiple_of(odd * ROWS, ROWS), ROWS)
    theirs = pl.ds(pl.multiple_of((1 - odd) * ROWS, ROWS), ROWS)
    own = pltpu.make_async_copy(blocks.at[0], rows_b.at[:, mine, :], own_sem)
    own.start()
    smalls = [
        pltpu.make_async_copy(src, dst, small_sem.at[i])
        for i, (src, dst) in enumerate(
            (
                (left_in, left), (right_in, right), (slices_in, slices),
                (weights_in, weights), (counts_in, counts), (subduction_in, subduction),
            )
        )
    ]
    for copy in smalls:
        copy.start()
    for copy in smalls:
        copy.wait()

    row = lax.broadcasted_iota(jnp.int32, (8, LANES), 0)
    keys = jnp.zeros((8, LANES), jnp.int32)
    coefs = jnp.zeros((8, LANES), jnp.float32)
    for s in range(PAIR_DEV):
        key = (slices[0, s] * FAM + right[0, s]) * FAM + left[0, s]
        coef = jnp.where(s < counts[0, 0], subduction[weights[0, s]], 0.0)
        keys = jnp.where(row == s, key, keys)
        coefs = jnp.where(row == 4 + s, coef, coefs)
    tile[...] = jnp.where(row < 4, keys.astype(jnp.float32), coefs)

    pl.semaphore_wait(barrier, len(friends))
    sends = []

    def send(src, dst, send_sem, recv_sem, to):
        copy = pltpu.make_async_remote_copy(
            src, dst, send_sem, recv_sem, device_id=to, device_id_type=MESH
        )
        copy.start()
        sends.append(copy)
        return copy

    for p in range(DEVS):
        send(tile, tiles.at[pair], tile_send.at[p], tile_recv.at[pair], (other, p))

    own.wait()
    gets_a, gets_relay, gets_b, gets_c = {}, {}, {}, {}
    for n, (first, width) in enumerate(CHUNKS):
        part = rows_b.at[:, mine, pl.ds(first, width)]
        send(part, part, b_send.at[n], b_recv.at[n], (mom, across))
        part = rows_b.at[:, theirs, pl.ds(first, width)]
        gets_b[n] = pltpu.make_async_copy(part, part, b_recv.at[n])

    for dx, dz in ((1, 1), (3, 1), (2, 1), (0, 1), (1, 0), (3, 0), (2, 0), (0, 0)):
        k = SLOT[dx, dz]
        columns = lax.div(at(dx, dz), 2) * LANES
        src = rows_b.at[:, mine, pl.ds(pl.multiple_of(columns, LANES), LANES)]
        if dx and dz:
            gets_relay[dx] = send(
                src, relay.at[dx - 1], a_send.at[k], relay_recv.at[dx - 1], (other, at(dx, 0))
            )
        else:
            gets_a[k] = send(
                src, parts_a.at[k], a_send.at[k], a_recv.at[k], (other, at(dx, dz))
            )
    place = lax.broadcasted_iota(jnp.int32, (MIX, LANES), 0) * FAM
    place = place + lax.div(lax.broadcasted_iota(jnp.int32, (MIX, LANES), 1), SUB)
    place_lo = place.astype(jnp.float32)
    place_hi = (place + LANES // SUB).astype(jnp.float32)
    lo = jnp.zeros((MIX, LANES), jnp.float32)
    hi = jnp.zeros((MIX, LANES), jnp.float32)
    for p in range(DEVS):
        pltpu.make_async_copy(tile, tiles.at[p], tile_recv.at[p]).wait()
    for p in range(DEVS):
        for s in range(PAIR_DEV):
            key = tiles[p, s : s + 1, :]
            coef = tiles[p, 4 + s : 5 + s, :]
            lo = lo + jnp.where(place_lo == key, coef, 0.0)
            hi = hi + jnp.where(place_hi == key, coef, 0.0)
    rest = jnp.concatenate([lo, hi], axis=1)
    diagonal = lax.broadcasted_iota(jnp.int32, (SUB, FAM * SUB), 0) == lax.rem(
        lax.broadcasted_iota(jnp.int32, (SUB, FAM * SUB), 1), SUB
    )
    for level in range(3):
        part = rest.astype(jnp.bfloat16).astype(jnp.float32)
        rest = rest - part
        spread[level] = part
    for level in range(3):
        for r in range(MIX):
            square = jnp.where(diagonal, spread[level, r : r + 1, :], 0.0)
            table[r * SUB : (r + 1) * SUB, level * FAM * SUB : (level + 1) * FAM * SUB] = (
                square.astype(jnp.bfloat16)
            )

    def combine(k):
        gets_a[k].wait_recv()

        @pl.loop(0, ROWS // (2 * SUB))
        def _(h):
            base = pl.multiple_of(h * 2 * SUB, 2 * SUB)
            both = parts_a[k, :, pl.ds(base, 2 * SUB), :]
            first = both[:, :SUB, :].reshape(FAM * SUB, LANES)
            second = both[:, SUB:, :].reshape(FAM * SUB, LANES)
            wide = jnp.concatenate([first, second], axis=1)
            mixed = jnp.dot(
                table[...],
                jnp.concatenate([wide, wide, wide], axis=0),
                preferred_element_type=jnp.float32,
            ).astype(jnp.bfloat16)
            for r in range(MIX):
                t, b = divmod(r, FAM)
                for e in range(2):
                    combined[
                        pl.ds(k * OUT_ROWS + t * ROWS + base + e * SUB, SUB),
                        b * LANES : (b + 1) * LANES,
                    ] = mixed[r * SUB : (r + 1) * SUB, e * LANES : (e + 1) * LANES]

    def pass_on(dx):
        k = SLOT[dx, 1]
        gets_relay[dx].wait_recv()
        gets_a[k] = send(
            relay.at[dx - 1], parts_a.at[k], relay_send.at[dx - 1], a_recv.at[k],
            (mom, at(0, 1)),
        )

    def multiply(n, k, count):
        first, width = CHUNKS[n]
        columns = slice(first, first + width)
        lines = slice(k * OUT_ROWS, (k + count) * OUT_ROWS)
        partial[lines, columns] = jnp.dot(
            combined[lines, :],
            rows_b[:, :, columns].reshape(FAM * LANES, width),
            preferred_element_type=jnp.float32,
        ).astype(jnp.bfloat16)
        for i in range(k, k + count):
            dx, dz = PEERS[i]
            gets_c[n, i] = send(
                partial.at[pl.ds(i * OUT_ROWS, OUT_ROWS), pl.ds(first, width)],
                landed.at[i, :, pl.ds(first, width)],
                c_send.at[n, i], c_recv.at[n, i], (other, at(-dx, dz)),
            )

    def finish(n):
        first, width = CHUNKS[n]
        columns = slice(first, first + width)
        total = jnp.zeros((OUT_ROWS, width), jnp.float32)
        for k in range(len(PEERS)):
            gets_c[n, k].wait_recv()
            total = total + landed[k, :, columns].astype(jnp.float32)
        for t in range(SLICES):
            out[:, t, columns] = total[t * ROWS : (t + 1) * ROWS, :]

    combine(SLOT[0, 0])
    pass_on(1)
    pass_on(3)
    combine(SLOT[0, 1])
    pass_on(2)
    gets_b[0].wait()
    multiply(0, 0, 2)
    for k in range(2, len(PEERS), 2):
        combine(k)
        combine(k + 1)
        multiply(0, k, 2)
    for n in range(1, len(CHUNKS)):
        gets_b[n].wait()
        for k in range(0, len(PEERS), DOT_ROWS // OUT_ROWS):
            multiply(n, k, DOT_ROWS // OUT_ROWS)
    for n in range(len(CHUNKS)):
        finish(n)
    for copy in sends:
        copy.wait_send()


def body(blocks, left_ids, right_ids, slice_ids, weight_ids, counts, subduction):
    bf16, f32 = jnp.bfloat16, jnp.float32
    peers, chunks = len(PEERS), len(CHUNKS)
    dma = pltpu.SemaphoreType.DMA
    result = pl.pallas_call(
        kernel,
        out_shape=jax.ShapeDtypeStruct((ROWS, SLICES, ORDER), f32),
        in_specs=[pl.BlockSpec(memory_space=pl.ANY)] * 7,
        out_specs=pl.BlockSpec(memory_space=pltpu.VMEM),
        scratch_shapes=[pltpu.SMEM((1, PAIR_DEV), jnp.int32)] * 4
        + [
            pltpu.SMEM((1, 1), jnp.int32),
            pltpu.SMEM(subduction.shape, f32),
            pltpu.VMEM((FAM, 2 * ROWS, ORDER), bf16),
            pltpu.VMEM((peers, FAM, ROWS, LANES), bf16),
            pltpu.VMEM((3, FAM, ROWS, LANES), bf16),
            pltpu.VMEM((peers * OUT_ROWS, FAM * LANES), bf16),
            pltpu.VMEM((peers * OUT_ROWS, ORDER), bf16),
            pltpu.VMEM((peers, OUT_ROWS, ORDER), bf16),
            pltpu.VMEM((MIX * SUB, 3 * FAM * SUB), bf16),
            pltpu.VMEM((8, LANES), f32),
            pltpu.VMEM((DEVS, 8, LANES), f32),
            pltpu.VMEM((3, MIX, FAM * SUB), f32),
            dma((6,)), dma, dma((DEVS,)), dma((DEVS,)), dma((peers,)), dma((peers,)),
            dma((3,)), dma((3,)), dma((chunks,)), dma((chunks,)),
            dma((chunks, peers)), dma((chunks, peers)),
        ],
        compiler_params=pltpu.CompilerParams(
            collective_id=0, has_side_effects=True, vmem_limit_bytes=60 << 20
        ),
        cost_estimate=pl.CostEstimate(
            flops=8 << 30, bytes_accessed=4 << 20, transcendentals=0
        ),
    )(left_ids, right_ids, slice_ids, weight_ids, counts, subduction, blocks)
    return result[None]


def solution(mesh):
    return jax.shard_map(
        body,
        mesh=mesh,
        in_specs=(
            P("mom", None, "pair", None),
            P("mom", "pair"),
            P("mom", "pair"),
            P("mom", "pair"),
            P("mom", "pair"),
            P("mom", "pair"),
            P(),
        ),
        out_specs=P("mom", "pair", None, None),
        check_vma=False,
    )
```

time: 74.3 us -> 66.5 us (0.90)
  Pallas kernels: 71.2 us -> 63.8 us
    pallas_call x1, Pallas kernels: 71.2 us -> 63.8 us  [body(): pl.pallas_call(kernel, out_shape=jax.ShapeDtypeStruct((ROWS, SLICES, ORDE...]
    reshape x1 -> x0, local copies, waits for them, and re-layouts: 2.24 us -> none  [body(): result = jnp.transpose(result.reshape(SLICES, ROWS, ORDER), (1, 0, 2))]
    unnamed x0 -> x1, local copies, waits for them, and re-layouts: none -> 1.87 us
where the time goes in v2:
time: 66.5 us; the launch traced here: 66.4 us
  Pallas kernels  63.8 us (96%)
  local copies, waits for them, and re-layouts  1.87 us (3%)
    pallas_call x1, Pallas kernels, body(): pl.pallas_call(kernel, out_shape=jax.ShapeDtypeStruct((ROWS, SLICES, ORDE...  63.8 us
    unnamed x1, local copies, waits for them, and re-layouts  1.87 us

profile of v2, /device:TPU:1, one launch (start us, length us, event | category | flops | bytes accessed | tf_op | source)
XLA Modules:
  0.0 66.4 jit_solution(15492404921654663034)
XLA Ops:
  0.7 63.8 %shard_map.73 = f32[64,2,1024]{2,1,0:T(2,128)} custom-call(s32[1,3]{1,0:T(1,128)} %left_in.1, s32[1,3]{1,0:T(1,128)} %right_in.1, s32[1,3]{1,0:T(1,128)} %slices_in.1, s32[1,3]{1,0:T(1,128)} %weights_in.1, s32[1,1]{1,0:T(1,128)S(6)} %copy.9.counts_in, f32[8]{0:T(128)} %subduction_in.1, bf16[1,16,64,1024]{3,2,1,0:T(8,128)(2,1)} %blocks.1), custom_call_target="tpu_custom_call" | custom-call | flops 8589934592 | bytes 4194304 | tf_op jit(solution)/shard_map/pallas_call | solution.py:225
  64.5 1.9 %copy.10 = f32[1,64,2,1024]{3,2,1,0:T(2,128)} copy(f32[1,64,2,1024]{3,2,1,0:T(2,128)} %bitcast.1) | data formatting | bytes 1048576

commit v3 on v2

--- a/solution.py
+++ b/solution.py
@@ -210,7 +210,7 @@
         multiply(0, k, 2)
     for n in range(1, len(CHUNKS)):
         gets_b[n].wait()
-        for k in range(0, len(PEERS), DOT_ROWS // OUT_ROWS):
+        for k in reversed(range(0, len(PEERS), DOT_ROWS // OUT_ROWS)):
             multiply(n, k, DOT_ROWS // OUT_ROWS)
     for n in range(len(CHUNKS)):
         finish(n)
@@ -224,7 +224,7 @@
     dma = pltpu.SemaphoreType.DMA
     result = pl.pallas_call(
         kernel,
-        out_shape=jax.ShapeDtypeStruct((ROWS, SLICES, ORDER), f32),
+        out_shape=pltpu.VMEM((ROWS, SLICES, ORDER), f32),
         in_specs=[pl.BlockSpec(memory_space=pl.ANY)] * 7,
         out_specs=pl.BlockSpec(memory_space=pltpu.VMEM),
         scratch_shapes=[pltpu.SMEM((1, PAIR_DEV), jnp.int32)] * 4
@@ -246,7 +246,7 @@
             dma((chunks, peers)), dma((chunks, peers)),
         ],
         compiler_params=pltpu.CompilerParams(
-            collective_id=0, has_side_effects=True, vmem_limit_bytes=60 << 20
+            collective_id=0, has_side_effects=True, vmem_limit_bytes=56 << 20
         ),
         cost_estimate=pl.CostEstimate(
             flops=8 << 30, bytes_accessed=4 << 20, transcendentals=0

time: 66.5 us -> 64.3 us (0.967)
  local copies, waits for them, and re-layouts: 1.87 us -> 0.8 us
  Pallas kernels: 63.8 us -> 62.8 us
    pallas_call x1, Pallas kernels: 63.8 us -> 62.8 us  [body(): pl.pallas_call(kernel, out_shape=pltpu.VMEM((ROWS, SLICES, ORDER), f32),...]
    unnamed x1, local copies, waits for them, and re-layouts: 1.87 us -> 0.8 us
where the time goes in v3:
time: 64.3 us; the launch traced here: 64.2 us
  Pallas kernels  62.8 us (98%)
  local copies, waits for them, and re-layouts  0.8 us (1%)
  between operations  0.66 us (1%)
    pallas_call x1, Pallas kernels, body(): pl.pallas_call(kernel, out_shape=pltpu.VMEM((ROWS, SLICES, ORDER), f32),...  62.8 us

profile of v3, /device:TPU:1, one launch (start us, length us, event | category | flops | bytes accessed | tf_op | source)
XLA Modules:
  0.0 64.2 jit_solution(10169574391917367044)
XLA Ops:
  0.7 62.8 %shard_map.73 = f32[64,2,1024]{2,1,0:T(2,128)S(1)} custom-call(s32[1,3]{1,0:T(1,128)} %left_in.1, s32[1,3]{1,0:T(1,128)} %right_in.1, s32[1,3]{1,0:T(1,128)} %slices_in.1, s32[1,3]{1,0:T(1,128)} %weights_in.1, s32[1,1]{1,0:T(1,128)S(6)} %copy.10.counts_in, f32[8]{0:T(128)} %subduction_in.1, bf16[1,16,64,1024]{3,2,1,0:T(8,128)(2,1)} %blocks.1), custom_call_target="tpu_custom_call" | custom-call | flops 8589934592 | bytes 4194304 | tf_op jit(solution)/shard_map/pallas_call | solution.py:225
  63.4 0.8 %copy.9 = f32[1,64,2,1024]{3,2,1,0:T(2,128)} copy(f32[1,64,2,1024]{3,2,1,0:T(2,128)S(1)} %bitcast.1) | data formatting | bytes 1048576

commit v4 on v3

--- a/solution.py
+++ b/solution.py
@@ -28,9 +28,9 @@
 def kernel(
     left_in, right_in, slices_in, weights_in, counts_in, subduction_in, blocks, out,
     left, right, slices, weights, counts, subduction,
-    rows_b, parts_a, relay, combined, partial, landed,
+    rows_own, rows_b, parts_a, relay, combined, partial, landed,
     table, tile, tiles, spread,
-    small_sem, own_sem, tile_send, tile_recv, a_send, a_recv, relay_send, relay_recv,
+    small_sem, own_sem, near_send, near_recv, tile_send, tile_recv, a_send, a_recv, relay_send, relay_recv,
     b_send, b_recv, c_send, c_recv,
 ):
     mom, pair = lax.axis_index("mom"), lax.axis_index("pair")
@@ -42,15 +42,15 @@
     def at(dx, dz):
         return lax.rem(x + dx + 4, 4) * 4 + (3 - z if dz else z)
 
-    friends = [(other, p) for p in range(DEVS)]
-    friends += [(mom, across), (mom, at(0, 1))]
+    friends = [(mom, lax.rem(pair + step, DEVS)) for step in range(1, DEVS)]
+    friends += [(other, pair), (other, across)]
     barrier = pltpu.get_barrier_semaphore()
     for friend in friends:
         pl.semaphore_signal(barrier, 1, device_id=friend, device_id_type=MESH)
 
     mine = pl.ds(pl.multiple_of(odd * ROWS, ROWS), ROWS)
     theirs = pl.ds(pl.multiple_of((1 - odd) * ROWS, ROWS), ROWS)
-    own = pltpu.make_async_copy(blocks.at[0], rows_b.at[:, mine, :], own_sem)
+    own = pltpu.make_async_copy(blocks.at[0], rows_own, own_sem)
     own.start()
     smalls = [
         pltpu.make_async_copy(src, dst, small_sem.at[i])
@@ -87,29 +87,43 @@
         sends.append(copy)
         return copy
 
-    for p in range(DEVS):
-        send(tile, tiles.at[pair], tile_send.at[p], tile_recv.at[pair], (other, p))
+    def keep(src, dst, sem):
+        copy = pltpu.make_async_copy(src, dst, sem)
+        copy.start()
+        return copy
+
+    for step in range(1, DEVS):
+        send(
+            tile, tiles.at[pair], tile_send.at[step], tile_recv.at[pair],
+            (mom, lax.rem(pair + step, DEVS)),
+        )
+    keep(tile, tiles.at[pair], tile_recv.at[pair])
 
     own.wait()
     gets_a, gets_relay, gets_b, gets_c = {}, {}, {}, {}
     for n, (first, width) in enumerate(CHUNKS):
-        part = rows_b.at[:, mine, pl.ds(first, width)]
-        send(part, part, b_send.at[n], b_recv.at[n], (mom, across))
-        part = rows_b.at[:, theirs, pl.ds(first, width)]
+        columns = pl.ds(first, width)
+        send(
+            rows_own.at[:, :, columns], rows_b.at[:, mine, columns], b_send.at[n],
+            b_recv.at[n], (other, across),
+        )
+        part = rows_b.at[:, theirs, columns]
         gets_b[n] = pltpu.make_async_copy(part, part, b_recv.at[n])
-
     for dx, dz in ((1, 1), (3, 1), (2, 1), (0, 1), (1, 0), (3, 0), (2, 0), (0, 0)):
         k = SLOT[dx, dz]
         columns = lax.div(at(dx, dz), 2) * LANES
-        src = rows_b.at[:, mine, pl.ds(pl.multiple_of(columns, LANES), LANES)]
+        src = rows_own.at[:, :, pl.ds(pl.multiple_of(columns, LANES), LANES)]
         if dx and dz:
             gets_relay[dx] = send(
-                src, relay.at[dx - 1], a_send.at[k], relay_recv.at[dx - 1], (other, at(dx, 0))
+                src, relay.at[dx - 1], a_send.at[k], relay_recv.at[dx - 1], (mom, at(dx, 0))
             )
+        elif dx or dz:
+            gets_a[k] = send(
+                src, parts_a.at[k], a_send.at[k], a_recv.at[k], (mom, at(dx, dz))
+            ).wait_recv
         else:
-            gets_a[k] = send(
-                src, parts_a.at[k], a_send.at[k], a_recv.at[k], (other, at(dx, dz))
-            )
+            gets_a[k] = keep(src, parts_a.at[k], a_recv.at[k]).wait
+    near = send(rows_own, rows_b.at[:, mine, :], near_send, near_recv, (other, pair))
     place = lax.broadcasted_iota(jnp.int32, (MIX, LANES), 0) * FAM
     place = place + lax.div(lax.broadcasted_iota(jnp.int32, (MIX, LANES), 1), SUB)
     place_lo = place.astype(jnp.float32)
@@ -140,7 +154,7 @@
             )
 
     def combine(k):
-        gets_a[k].wait_recv()
+        gets_a[k]()
 
         @pl.loop(0, ROWS // (2 * SUB))
         def _(h):
@@ -168,7 +182,7 @@
         gets_a[k] = send(
             relay.at[dx - 1], parts_a.at[k], relay_send.at[dx - 1], a_recv.at[k],
             (mom, at(0, 1)),
-        )
+        ).wait_recv
 
     def multiply(n, k, count):
         first, width = CHUNKS[n]
@@ -181,18 +195,21 @@
         ).astype(jnp.bfloat16)
         for i in range(k, k + count):
             dx, dz = PEERS[i]
-            gets_c[n, i] = send(
-                partial.at[pl.ds(i * OUT_ROWS, OUT_ROWS), pl.ds(first, width)],
-                landed.at[i, :, pl.ds(first, width)],
-                c_send.at[n, i], c_recv.at[n, i], (other, at(-dx, dz)),
-            )
+            src = partial.at[pl.ds(i * OUT_ROWS, OUT_ROWS), pl.ds(first, width)]
+            dst = landed.at[i, :, pl.ds(first, width)]
+            if dx or dz:
+                gets_c[n, i] = send(
+                    src, dst, c_send.at[n, i], c_recv.at[n, i], (mom, at(-dx, dz))
+                ).wait_recv
+            else:
+                gets_c[n, i] = keep(src, dst, c_recv.at[n, i]).wait
 
     def finish(n):
         first, width = CHUNKS[n]
         columns = slice(first, first + width)
         total = jnp.zeros((OUT_ROWS, width), jnp.float32)
         for k in range(len(PEERS)):
-            gets_c[n, k].wait_recv()
+            gets_c[n, k]()
             total = total + landed[k, :, columns].astype(jnp.float32)
         for t in range(SLICES):
             out[:, t, columns] = total[t * ROWS : (t + 1) * ROWS, :]
@@ -202,6 +219,7 @@
     pass_on(3)
     combine(SLOT[0, 1])
     pass_on(2)
+    near.wait_recv()
     gets_b[0].wait()
     multiply(0, 0, 2)
     for k in range(2, len(PEERS), 2):
@@ -231,6 +249,7 @@
         + [
             pltpu.SMEM((1, 1), jnp.int32),
             pltpu.SMEM(subduction.shape, f32),
+            pltpu.VMEM((FAM, ROWS, ORDER), bf16),
             pltpu.VMEM((FAM, 2 * ROWS, ORDER), bf16),
             pltpu.VMEM((peers, FAM, ROWS, LANES), bf16),
             pltpu.VMEM((3, FAM, ROWS, LANES), bf16),
@@ -241,7 +260,7 @@
             pltpu.VMEM((8, LANES), f32),
             pltpu.VMEM((DEVS, 8, LANES), f32),
             pltpu.VMEM((3, MIX, FAM * SUB), f32),
-            dma((6,)), dma, dma((DEVS,)), dma((DEVS,)), dma((peers,)), dma((peers,)),
+            dma((6,)), dma, dma, dma, dma((DEVS,)), dma((DEVS,)), dma((peers,)), dma((peers,)),
             dma((3,)), dma((3,)), dma((chunks,)), dma((chunks,)),
             dma((chunks, peers)), dma((chunks, peers)),
         ],

time: 64.3 us -> 63.4 us (0.986)
  Pallas kernels: 62.8 us -> 61.8 us
    pallas_call x1, Pallas kernels: 62.8 us -> 61.8 us  [body(): pl.pallas_call(kernel, out_shape=pltpu.VMEM((ROWS, SLICES, ORDER), f32),...]
where the time goes in v4:
time: 63.4 us; the launch traced here: 63.3 us
  Pallas kernels  61.8 us (97%)
  local copies, waits for them, and re-layouts  0.8 us (1%)
  between operations  0.66 us (1%)
    pallas_call x1, Pallas kernels, body(): pl.pallas_call(kernel, out_shape=pltpu.VMEM((ROWS, SLICES, ORDER), f32),...  61.8 us

profile of v4, /device:TPU:1, one launch (start us, length us, event | category | flops | bytes accessed | tf_op | source)
XLA Modules:
  0.0 63.3 jit_solution(11285415070398167384)
XLA Ops:
  0.7 61.8 %shard_map.73 = f32[64,2,1024]{2,1,0:T(2,128)S(1)} custom-call(s32[1,3]{1,0:T(1,128)} %left_in.1, s32[1,3]{1,0:T(1,128)} %right_in.1, s32[1,3]{1,0:T(1,128)} %slices_in.1, s32[1,3]{1,0:T(1,128)} %weights_in.1, s32[1,1]{1,0:T(1,128)S(6)} %copy.10.counts_in, f32[8]{0:T(128)} %subduction_in.1, bf16[1,16,64,1024]{3,2,1,0:T(8,128)(2,1)} %blocks.1), custom_call_target="tpu_custom_call" | custom-call | flops 8589934592 | bytes 4194304 | tf_op jit(solution)/shard_map/pallas_call | solution.py:243
  62.5 0.8 %copy.9 = f32[1,64,2,1024]{3,2,1,0:T(2,128)} copy(f32[1,64,2,1024]{3,2,1,0:T(2,128)S(1)} %bitcast.1) | data formatting | bytes 1048576

commit v5 on v4

--- a/solution.py
+++ b/solution.py
@@ -226,9 +226,14 @@
         combine(k)
         combine(k + 1)
         multiply(0, k, 2)
+        if k == 4:
+            gets_b[1].wait()
+            multiply(1, 0, 2)
+            multiply(1, 2, 2)
     for n in range(1, len(CHUNKS)):
-        gets_b[n].wait()
-        for k in reversed(range(0, len(PEERS), DOT_ROWS // OUT_ROWS)):
+        if n > 1:
+            gets_b[n].wait()
+        for k in reversed(range(0 if n > 1 else 4, len(PEERS), DOT_ROWS // OUT_ROWS)):
             multiply(n, k, DOT_ROWS // OUT_ROWS)
     for n in range(len(CHUNKS)):
         finish(n)

time: 63.4 us -> 63.4 us (level)
  no operation moved by 1% of the time
where the time goes in v5:
time: 63.4 us; the launch traced here: 63.3 us
  Pallas kernels  61.8 us (97%)
  local copies, waits for them, and re-layouts  0.8 us (1%)
  between operations  0.66 us (1%)
    pallas_call x1, Pallas kernels, body(): pl.pallas_call(kernel, out_shape=pltpu.VMEM((ROWS, SLICES, ORDER), f32),...  61.8 us

profile of v5, /device:TPU:1, one launch (start us, length us, event | category | flops | bytes accessed | tf_op | source)
XLA Modules:
  0.0 63.3 jit_solution(16552470690203272380)
XLA Ops:
  0.7 61.8 %shard_map.73 = f32[64,2,1024]{2,1,0:T(2,128)S(1)} custom-call(s32[1,3]{1,0:T(1,128)} %left_in.1, s32[1,3]{1,0:T(1,128)} %right_in.1, s32[1,3]{1,0:T(1,128)} %slices_in.1, s32[1,3]{1,0:T(1,128)} %weights_in.1, s32[1,1]{1,0:T(1,128)S(6)} %copy.10.counts_in, f32[8]{0:T(128)} %subduction_in.1, bf16[1,16,64,1024]{3,2,1,0:T(8,128)(2,1)} %blocks.1), custom_call_target="tpu_custom_call" | custom-call | flops 8589934592 | bytes 4194304 | tf_op jit(solution)/shard_map/pallas_call | solution.py:248
  62.5 0.8 %copy.9 = f32[1,64,2,1024]{3,2,1,0:T(2,128)} copy(f32[1,64,2,1024]{3,2,1,0:T(2,128)S(1)} %bitcast.1) | data formatting | bytes 1048576
